TPU v7x, 32 devices: a whole 2x2x4 slice. The times are simulated.
32 devices in a mesh: gx: 8 (over z, core), gy: 4 (over y, x).
Axes of the slice: x: 2, y: 2, z: 4, core: 2. Of those that a mesh axis runs over, the one named last changes fastest.
Arguments:
- member_flows: float32 [24, 4, 64, 32, 128], P(None, None, 'gx', 'gy'), may hold values from -6 to 6
- wall_texture: float32 [24, 64, 32], P(None, 'gx', 'gy'), may hold values from 0.2 to 2
- cross_link_matrix: float32 [4, 4], replicated, may hold values from -3 to 3
- obs_owner: int32 [4, 4096], replicated, may hold values from 0 to 31
- obs_cell: int32 [4, 4096], replicated, may hold values from 0 to 8191
- obs_value: float32 [4, 4096], replicated, may hold values from -8 to 8
- obs_var: float32 [4, 4096], replicated, may hold values from 0.1 to 1
- local_mask: int32 [4, 8, 4, 64], P(None, 'gx', 'gy'), may hold values 0 or 1
Outputs:
- analysis: float32 [24, 4, 64, 32, 128], P(None, None, 'gx', 'gy')
- rough_post: float32 [24, 64, 32], P(None, 'gx', 'gy')
Inputs may be any that keep to these rules, and one draw needn't show every extreme that they name: `obs_owner`: observations are skewed towards a few tiles.
All inputs are finite; a program needn't handle non-finite values. No bound on the sum of `local_mask` on one device may be relied on, other than what follows from the above.
Results may differ from a plain program's by a relative error of at most 0.0003.
Values sent between devices are 32-bit elements; how exact they have to be, the bound alone decides.
A program may use at most 64 MiB of HBM per device.

v0:
```python
import jax
import jax.numpy as jnp
from jax import lax
from jax.sharding import PartitionSpec as P

BATCHES = 4
OBS_BLOCK = 64


def padded_2(block, sides, width):
    for axis, dim in sides:
        count = lax.axis_size(axis)
        forward = [(i, i + 1) for i in range(count - 1)]
        backward = [(target, source) for source, target in forward]
        low = lax.ppermute(
            lax.slice_in_dim(block, block.shape[dim] - width, None, axis=dim), axis, forward
        )
        high = lax.ppermute(lax.slice_in_dim(block, 0, width, axis=dim), axis, backward)
        block = jnp.concatenate([low, block, high], axis=dim)
    return block


def prior_flow_vector(member_flow_vector, wall_texture_entries, cross_link_matrix):
    padded = padded_2(member_flow_vector, (("gx", 2), ("gy", 3)), 1)
    padded = jnp.pad(padded, ((0, 0), (0, 0), (0, 0), (0, 0), (1, 1)))
    center = padded[:, :, 1:-1, 1:-1, 1:-1]
    lap = padded[:, :, 2:, 1:-1, 1:-1] + padded[:, :, :-2, 1:-1, 1:-1]
    lap = lap + padded[:, :, 1:-1, 2:, 1:-1] + padded[:, :, 1:-1, :-2, 1:-1]
    lap = lap + padded[:, :, 1:-1, 1:-1, 2:] + padded[:, :, 1:-1, 1:-1, :-2] - 6.0 * center
    slope = 0.5 * (padded[:, :, 2:, 1:-1, 1:-1] - padded[:, :, :-2, 1:-1, 1:-1])
    mixed = jnp.einsum(
        "fg,mgxyz->mfxyz", cross_link_matrix, center, precision=lax.Precision.HIGHEST
    )
    level = (lax.broadcasted_iota(jnp.int32, (center.shape[-1],), 0) == 0).astype(jnp.float32)
    drag = wall_texture_entries[:, None, :, :, None] * center * level
    return center + 0.5 * (0.15 * lap - 0.6 * slope + mixed - drag)


def observation_terms(values, value_b, var_b):
    members = values.shape[0]
    ybar = jnp.mean(values, axis=0)
    dev = values - ybar[None, :]
    spread = jnp.sum(dev * dev, axis=0) / (members - 1.0)
    root = jnp.sqrt(spread + var_b)
    gterm = ((value_b - ybar) / (spread + var_b))[None, :] - dev / (
        root * (jnp.sqrt(var_b) + root)
    )[None, :]
    return (dev, gterm)


def apply_mixing(member_flow_vector, wall_texture_entries, mixing):
    flat_state = member_flow_vector.reshape(member_flow_vector.shape[0], -1)
    prime = flat_state - jnp.mean(flat_state, axis=0, keepdims=True)
    member_flow_vector = (
        flat_state + jnp.dot(mixing.T, prime, precision=lax.Precision.HIGHEST)
    ).reshape(member_flow_vector.shape)
    flat_rough = wall_texture_entries.reshape(wall_texture_entries.shape[0], -1)
    rprime = flat_rough - jnp.mean(flat_rough, axis=0, keepdims=True)
    wall_texture_entries = (
        flat_rough + jnp.dot(mixing.T, rprime, precision=lax.Precision.HIGHEST)
    ).reshape(wall_texture_entries.shape)
    return (member_flow_vector, wall_texture_entries)


def on_device(
    member_flows,
    wall_texture,
    cross_link_matrix,
    obs_owner,
    obs_cell,
    obs_value,
    obs_var,
    local_mask,
):
    members = member_flows.shape[0]
    cells = member_flows.shape[2] * member_flows.shape[3] * member_flows.shape[4]
    member_flow_vector = prior_flow_vector(member_flows, wall_texture, cross_link_matrix)
    wall_texture_entries = wall_texture
    mytile = lax.axis_index("gx") * lax.axis_size("gy") + lax.axis_index("gy")
    for batch in range(BATCHES):
        flat_first = member_flow_vector[:, 0].reshape(members, cells)
        picked = jnp.take(flat_first, obs_cell[batch], axis=1)
        owned = (obs_owner[batch] == mytile)[None, :]
        local_vals = jnp.where(owned, picked, 0.0)
        block_weight = local_mask[batch, 0, 0].astype(jnp.float32)
        values = lax.psum(local_vals, ("gx", "gy"))
        dev, gterm = observation_terms(values, obs_value[batch], obs_var[batch])
        weighted = dev * jnp.repeat(block_weight, OBS_BLOCK)[None, :]
        mixing = jnp.dot(weighted, gterm.T, precision=lax.Precision.HIGHEST) / (members - 1.0)
        member_flow_vector, wall_texture_entries = apply_mixing(
            member_flow_vector, wall_texture_entries, mixing
        )
    return (member_flow_vector, wall_texture_entries)


def solution(mesh):
    return jax.shard_map(
        on_device,
        mesh=mesh,
        in_specs=(
            P(None, None, "gx", "gy", None),
            P(None, "gx", "gy"),
            P(),
            P(),
            P(),
            P(),
            P(),
            P(None, "gx", "gy", None),
        ),
        out_specs=(P(None, None, "gx", "gy", None), P(None, "gx", "gy")),
        check_vma=False,
    )
```

profile of v0, /device:TPU:0, one launch (start us, length us, event | category | flops | bytes accessed | tf_op | source)
XLA Modules:
  0.0 787.6 jit_solution(4160225619469467906)
XLA Ops:
  7.3 4.5 copy.87
  14.4 3.1 collective-permute-start.1
  22.1 2.7 constant_dynamic-update-slice_fusion.1
  29.2 4.9 collective-permute-start.3
  37.4 4.0 collective-permute-done.2
  43.1 9.1 %select_maximum_fusion = f32[24,4,10,10,130]{4,1,3,2,0:T(4,128)S(1)} fusion(f32[24,4,10,1,128]{4,1,3,2,0:T(4,128)S(1)} %collective-permute-done.2, f32[24,4,10,8,128]{4,1,3,2,0:T(4,128)} %copy-done.9, f32[24,4,10,1,128]{4,1,3,2,0:T(4,128)S(1)} %collective-permute-done.3), kind=kLoop, calls=%fused_computation.10 | loop fusion | flops 9984000 | bytes 9907200 | tf_op jit(solution)/shard_map/concatenate | solution.py:19
  52.3 13.3 %fusion.94 = (f32[4,8,8,128]{3,0,2,1:T(4,128)S(1)}, f32[24,4,8,8,128]{4,1,3,2,0:T(4,128)S(1)}) fusion(f32[24,4,8,8,128]{4,1,3,2,0:T(4,128)S(1)} %copy-done.12, f32[128]{0:T(128)S(1)} %compare_convert_fusion, f32[24,8,8]{2,1,0:T(8,128)S(1)} %copy.85, f32[4,4]{1,0:T(4,128)S(1)} %copy-done, f32[24,4,10,10,130]{4,1,3,2,0:T(4,128)S(1)} %select_maximum_fusion, ...), kind=kOutput, calls=%fused_computation.155 | convolution fusion | flops 55017472 | bytes 21662208 | tf_op jit(solution)/shard_map/fg,mgxyz->mfxyz/dot_general | solution.py:31
  67.7 4.6 copy.97
  72.3 16.4 %gather_fusion = f32[4096,24]{1,0:T(8,128)} fusion(f32[24,8192]{0,1:T(8,128)} %bitcast.91, s32[4096]{0:T(1024)S(1)} %fusion.79), kind=kCustom, calls=%fused_computation.clone | custom fusion | bytes 802816 | tf_op jit(solution)/shard_map/jit(_take)/gather | solution.py:82
  88.7 6.0 bitcast_select_fusion.3
  94.9 148.3 %all-reduce.6.cloned.1.call-done = f32[24,4096]{0,1:T(8,128)} async-done(((f32[24,4096]{0,1:T(8,128)}), f32[24,4096]{0,1:T(8,128)}) %all-reduce.6.cloned.1.call-update) | async-done | bytes 393232 | tf_op jit(solution)/shard_map/psum | solution.py:86
  245.4 2.5 multiply_reduce_fusion.3
  248.9 8.3 %fusion.41 = f32[24,24]{1,0:T(8,128)S(1)} fusion(f32[24,4096]{0,1:T(8,128)} %all-reduce.6.cloned.1.call-done, f32[4096]{0:T(1024)S(1)} %bitcast.120, f32[4096]{0:T(1024)S(1)} %bitcast.119, f32[4096]{0:T(1024)S(1)} %mul.121, f32[4096]{0:T(1024)S(1)} %broadcast_multiply_fusion.10), kind=kOutput, calls=%fused_computation.70 | convolution fusion | flops 28803648 | bytes 461056 | tf_op jit(solution)/shard_map/dot_general | solution.py:89
  257.2 6.3 fusion.95
  265.3 2.6 copy.91
  267.9 13.0 %gather_fusion.1 = f32[4096,24]{1,0:T(8,128)S(1)} fusion(f32[24,8192]{0,1:T(8,128)} %bitcast.92, s32[4096]{0:T(1024)S(1)} %fusion.80), kind=kCustom, calls=%fused_computation.1.clone | custom fusion | bytes 802816 | tf_op jit(solution)/shard_map/jit(_take)/gather | solution.py:82
  280.9 2.7 bitcast_select_fusion.2
  284.7 131.7 %all-reduce.8.cloned.1.call-done = f32[24,4096]{0,1:T(8,128)} async-done(((f32[24,4096]{0,1:T(8,128)}), f32[24,4096]{0,1:T(8,128)}) %all-reduce.8.cloned.1.call-update) | async-done | bytes 393232 | tf_op jit(solution)/shard_map/psum | solution.py:86
  421.1 6.2 fusion.46
  427.4 3.4 fusion.96
  432.3 3.6 copy.92
  435.9 16.4 %gather_fusion.2 = f32[4096,24]{1,0:T(8,128)} fusion(f32[24,8192]{0,1:T(8,128)} %bitcast.93, s32[4096]{0:T(1024)S(1)} %fusion.81), kind=kCustom, calls=%fused_computation.2.clone | custom fusion | bytes 802816 | tf_op jit(solution)/shard_map/jit(_take)/gather | solution.py:82
  452.2 6.0 bitcast_select_fusion.1
  458.8 132.2 %all-reduce.10.cloned.1.call-done = f32[24,4096]{0,1:T(8,128)} async-done(((f32[24,4096]{0,1:T(8,128)}), f32[24,4096]{0,1:T(8,128)}) %all-reduce.10.cloned.1.call-update) | async-done | bytes 393232 | tf_op jit(solution)/shard_map/psum | solution.py:86
  596.7 8.3 %fusion.51 = f32[24,24]{1,0:T(8,128)S(1)} fusion(f32[24,4096]{0,1:T(8,128)} %all-reduce.10.cloned.1.call-done, f32[4096]{0:T(1024)S(1)} %bitcast.124, f32[4096]{0:T(1024)S(1)} %bitcast.123, f32[4096]{0:T(1024)} %mul.131, f32[4096]{0:T(1024)S(1)} %broadcast_multiply_fusion.8), kind=kOutput, calls=%fused_computation.72 | convolution fusion | flops 28803648 | bytes 461056 | tf_op jit(solution)/shard_map/dot_general | solution.py:89
  605.1 3.4 fusion.97
  610.2 2.6 copy.93
  612.8 13.0 %gather_fusion.3 = f32[4096,24]{1,0:T(8,128)S(1)} fusion(f32[24,8192]{0,1:T(8,128)} %bitcast.94, s32[4096]{0:T(1024)S(1)} %fusion.82), kind=kCustom, calls=%fused_computation.3.clone | custom fusion | bytes 802816 | tf_op jit(solution)/shard_map/jit(_take)/gather | solution.py:82
  625.8 2.7 bitcast_select_fusion
  628.7 132.5 %all-reduce.12.cloned.1.call-done = f32[24,4096]{0,1:T(8,128)} async-done(((f32[24,4096]{0,1:T(8,128)}), f32[24,4096]{0,1:T(8,128)}) %all-reduce.12.cloned.1.call-update) | async-done | bytes 393232 | tf_op jit(solution)/shard_map/psum | solution.py:86
  766.0 8.8 %fusion.56 = f32[24,24]{1,0:T(8,128)S(1)} fusion(f32[24,4096]{0,1:T(8,128)} %all-reduce.12.cloned.1.call-done, f32[4096]{0:T(1024)S(1)} %bitcast.126, f32[4096]{0:T(1024)S(1)} %bitcast.125, f32[4096]{0:T(1024)S(1)} %copy-done.20, f32[4096]{0:T(1024)S(1)} %broadcast_multiply_fusion.7), kind=kOutput, calls=%fused_computation.73 | convolution fusion | flops 28803648 | bytes 461056 | tf_op jit(solution)/shard_map/dot_general | solution.py:89
  775.6 3.1 fusion.34
  (140 shorter events, 46.9 us)
Async XLA Ops:
  7.2 45.1 %copy-start = (f32[4,4]{1,0:T(4,128)S(1)}, f32[4,4]{1,0:T(4,128)}, u32[]{:S(2)}) copy-start(f32[4,4]{1,0:T(4,128)} %param.12) | copy-start | bytes 196
  7.2 14.9 %copy-start.6 = (f32[24,4,8,8,128]{4,3,2,1,0:T(8,128)S(1)}, f32[24,4,8,8,128]{4,3,2,1,0:T(8,128)}, u32[]{:S(2)}) copy-start(f32[24,4,8,8,128]{4,3,2,1,0:T(8,128)} %param.10) | copy-start | bytes 9437188
  7.2 11.6 %copy-start.15 = (s32[4,4096]{1,0:T(4,128)S(1)}, s32[4,4096]{1,0:T(4,128)}, u32[]{:S(2)}) copy-start(s32[4,4096]{1,0:T(4,128)} %param.14) | copy-start | bytes 196612
  7.2 11.7 %copy-start.13 = (f32[24,8,8]{0,2,1:T(8,128)S(1)}, f32[24,8,8]{0,2,1:T(8,128)}, u32[]{:S(2)}) copy-start(f32[24,8,8]{0,2,1:T(8,128)} %param.11) | copy-start | bytes 18436
  7.2 13.0 %copy-start.28 = (s32[4,1,1,64]{3,2,1,0:T(1,128)S(1)}, s32[4,1,1,64]{3,2,1,0:T(1,128)}, u32[]{:S(2)}) copy-start(s32[4,1,1,64]{3,2,1,0:T(1,128)} %param.17) | copy-start | bytes 3076
  7.2 13.0 %copy-start.14 = (s32[4,4096]{1,0:T(4,128)S(1)}, s32[4,4096]{1,0:T(4,128)}, u32[]{:S(2)}) copy-start(s32[4,4096]{1,0:T(4,128)} %param.13) | copy-start | bytes 196612
  7.2 236.0 %all-reduce.6.cloned.1.call-start = ((), (), s32[]{:S(2)}) async-start(), calls=%async_computation | async-start | bytes 4194304 | tf_op jit(solution)/shard_map/psum | solution.py:86
  14.4 6.6 collective-permute-start.1
  17.5 7.3 collective-permute-start
  27.9 13.4 %collective-permute-start.2 = (f32[24,4,10,1,128]{4,1,3,2,0:T(4,128)S(1)}, f32[24,4,10,1,128]{4,1,3,2,0:T(4,128)S(1)}, u32[]{:S(2)}, u32[]{:S(2)}) collective-permute-start(f32[24,4,10,1,128]{4,1,3,2,0:T(4,128)S(1)} %get-tuple-element.10), channel_id=1, source_target_pairs={{1,0},{2,1},{3,2},{5,4},{6,5},{7,6},{9,8},{10,9},{11,10},{13,12},{... | collective-permute-start | bytes 1474568 | tf_op jit(solution)/shard_map/ppermute | solution.py:18
  29.2 13.9 %collective-permute-start.3 = (f32[24,4,10,1,128]{4,1,3,2,0:T(4,128)S(1)}, f32[24,4,10,1,128]{4,1,3,2,0:T(4,128)S(1)}, u32[]{:S(2)}, u32[]{:S(2)}) collective-permute-start(f32[24,4,10,1,128]{4,1,3,2,0:T(4,128)S(1)} %get-tuple-element.9), channel_id=1, source_target_pairs={{0,1},{1,2},{2,3},{4,5},{5,6},{6,7},{8,9},{9,10},{10,11},{12,13},{... | collective-permute-start | bytes 1474568 | tf_op jit(solution)/shard_map/ppermute | solution.py:15
  37.4 14.9 %copy-start.10 = (f32[24,4,10,8,128]{4,1,3,2,0:T(4,128)S(1)}, f32[24,4,10,8,128]{4,1,3,2,0:T(4,128)}, u32[]{:S(2)}) copy-start(f32[24,4,10,8,128]{4,1,3,2,0:T(4,128)} %copy-done.9) | copy-start | bytes 11796484
  37.4 14.9 %copy-start.12 = (f32[24,4,8,8,128]{4,1,3,2,0:T(4,128)S(1)}, f32[24,4,8,8,128]{4,1,3,2,0:T(4,128)}, u32[]{:S(2)}) copy-start(f32[24,4,8,8,128]{4,1,3,2,0:T(4,128)} %copy-done.11) | copy-start | bytes 9437188
  94.6 321.8 %all-reduce.8.cloned.1.call-start = ((), (), s32[]{:S(2)}) async-start(), calls=%async_computation.1 | async-start | bytes 4194304 | tf_op jit(solution)/shard_map/psum | solution.py:86
  257.2 6.3 copy-start.18
  265.3 15.6 %copy-start.26 = (pred[4096]{0:T(1024)(128)(4,1)S(1)}, pred[4096]{0:T(1024)(128)(4,1)}, u32[]{:S(2)}) copy-start(pred[4096]{0:T(1024)(128)(4,1)} %get-tuple-element.6) | copy-start | bytes 12292
  280.9 3.0 copy-start.19
  280.9 3.0 copy-start.27
  283.5 136.6 %copy-start.16 = (f32[4,4096]{1,0:T(4,128)S(1)}, f32[4,4096]{1,0:T(4,128)}, u32[]{:S(2)}) copy-start(f32[4,4096]{1,0:T(4,128)} %param.15) | copy-start | bytes 196612
  283.6 137.5 %copy-start.21 = (f32[4096]{0:T(1024)S(1)}, f32[4096]{0:T(1024)}, u32[]{:S(2)}) copy-start(f32[4096]{0:T(1024)} %mul.126) | copy-start | bytes 49156
  283.6 307.5 %all-reduce.10.cloned.1.call-start = ((), (), s32[]{:S(2)}) async-start(), calls=%async_computation.2 | async-start | bytes 4194304 | tf_op jit(solution)/shard_map/psum | solution.py:86
  416.4 2.4 copy-start.7
  421.1 6.3 copy-start.3
  432.3 19.9 %copy-start.24 = (pred[4096]{0:T(1024)(128)(4,1)S(1)}, pred[4096]{0:T(1024)(128)(4,1)}, u32[]{:S(2)}) copy-start(pred[4096]{0:T(1024)(128)(4,1)} %compare_and_fusion.1) | copy-start | bytes 12292
  432.3 19.9 %copy-start.25 = (pred[4096]{0:T(1024)(128)(4,1)S(1)}, pred[4096]{0:T(1024)(128)(4,1)}, u32[]{:S(2)}) copy-start(pred[4096]{0:T(1024)(128)(4,1)} %get-tuple-element.8) | copy-start | bytes 12292
  452.2 6.3 copy-start.17
  458.2 303.0 %all-reduce.12.cloned.1.call-start = ((), (), s32[]{:S(2)}) async-start(), calls=%async_computation.3 | async-start | bytes 4194304 | tf_op jit(solution)/shard_map/psum | solution.py:86
  610.2 15.6 %copy-start.22 = (pred[4096]{0:T(1024)(128)(4,1)S(1)}, pred[4096]{0:T(1024)(128)(4,1)}, u32[]{:S(2)}) copy-start(pred[4096]{0:T(1024)(128)(4,1)} %compare_and_fusion) | copy-start | bytes 12292
  610.2 15.6 %copy-start.23 = (pred[4096]{0:T(1024)(128)(4,1)S(1)}, pred[4096]{0:T(1024)(128)(4,1)}, u32[]{:S(2)}) copy-start(pred[4096]{0:T(1024)(128)(4,1)} %get-tuple-element.5) | copy-start | bytes 12292
  628.5 137.5 %copy-start.20 = (f32[4096]{0:T(1024)S(1)}, f32[4096]{0:T(1024)}, u32[]{:S(2)}) copy-start(f32[4096]{0:T(1024)} %mul.136) | copy-start | bytes 49156
  765.9 9.7 %copy-start.5 = (f32[24,32768]{1,0:T(8,128)S(1)}, f32[24,32768]{1,0:T(8,128)}, u32[]{:S(2)}) copy-start(f32[24,32768]{1,0:T(8,128)} %copy-done.4) | copy-start | bytes 9437188
  775.6 5.3 copy-start.1
  (5 other events, 9.2 us)
Sparse Core Ops, SparseCore 0:
  94.8 148.4 all-reduce.5
  283.7 132.6 all-reduce.7
  458.4 132.6 all-reduce.9
  628.6 132.6 all-reduce.11
where the time goes:
time: 797 us; the launch traced here: 788 us
  waiting for transfers between devices  551 us (69%)
  local copies, waits for them, and re-layouts  99.2 us (12%)
  matrix products  62.7 us (8%)
  other arithmetic  49.2 us (6%)
  between operations  14.7 us (2%)
  starting transfers between devices  11.4 us (1%)
    psum x4, waiting for transfers between devices, on_device(): values = lax.psum(local_vals, ('gx', 'gy'))  545 us
    gather x4, local copies, waits for them, and re-layouts, on_device(): picked = jnp.take(flat_first, obs_cell[batch], axis=1)  58.7 us
    dot_general x4, matrix products, on_device(): jnp.dot(weighted, gterm.T, precision=lax.Precision.HIGHEST)  31.6 us
    unnamed x66, local copies, waits for them, and re-layouts  18.1 us
    select_n x4, other arithmetic, on_device(): local_vals = jnp.where(owned, picked, 0.0)  17.3 us
    dot_general x4, matrix products, apply_mixing(): jnp.dot(mixing.T, prime, precision=lax.Precision.HIGHEST)  16.2 us
  transfers between devices with their start and end apart: 8, of which 6 were waited for; matrix products, arithmetic and copies ran while one was open for 1% of the time, Pallas kernels for 0%

commit v1 on v0

--- a/solution.py
+++ b/solution.py
@@ -2,6 +2,7 @@
 import jax.numpy as jnp
 from jax import lax
 from jax.sharding import PartitionSpec as P
+from jax.lax import all_gather
 
 BATCHES = 4
 OBS_BLOCK = 64
@@ -83,7 +84,7 @@
         owned = (obs_owner[batch] == mytile)[None, :]
         local_vals = jnp.where(owned, picked, 0.0)
         block_weight = local_mask[batch, 0, 0].astype(jnp.float32)
-        values = lax.psum(local_vals, ("gx", "gy"))
+        values = all_gather(local_vals, ("gx", "gy")).sum(axis=0)
         dev, gterm = observation_terms(values, obs_value[batch], obs_var[batch])
         weighted = dev * jnp.repeat(block_weight, OBS_BLOCK)[None, :]
         mixing = jnp.dot(weighted, gterm.T, precision=lax.Precision.HIGHEST) / (members - 1.0)

time: 797 us -> 663 us (0.83)
  waiting for transfers between devices: 551 us -> 392 us
  other arithmetic: 49.2 us -> 81 us
  matrix products: 62.7 us -> 40.3 us
  local copies, waits for them, and re-layouts: 99.2 us -> 115 us
    psum x4 -> x0, waiting for transfers between devices: 545 us -> none  [on_device(): values = lax.psum(local_vals, ('gx', 'gy'))]
    all_gather x0 -> x4, waiting for transfers between devices: none -> 384 us  [on_device(): values = all_gather(local_vals, ('gx', 'gy')).sum(axis=0)]
    dot_general x4, matrix products: 31.6 us -> 4.51 us  [on_device(): jnp.dot(weighted, gterm.T, precision=lax.Precision.HIGHEST)]
    reduce_sum x0 -> x4, other arithmetic: none -> 20.8 us  [on_device(): values = all_gather(local_vals, ('gx', 'gy')).sum(axis=0)]
    reduce_sum x4, other arithmetic: 9.09 us -> 22.1 us  [observation_terms(): ybar = jnp.mean(values, axis=0)]
    unnamed x66 -> x74, local copies, waits for them, and re-layouts: 18.1 us -> 20.1 us
  transfers between devices with their start and end apart: 8 -> 8, of which waited for: 6 -> 6; matrix products, arithmetic and copies ran while one was open for 1% -> 2% of each run, Pallas kernels for 0% -> 0%
where the time goes in v1:
time: 663 us; the launch traced here: 653 us
  waiting for transfers between devices  392 us (59%)
  local copies, waits for them, and re-layouts  115 us (17%)
  other arithmetic  81 us (12%)
  matrix products  40.3 us (6%)
  between operations  14.7 us (2%)
  starting transfers between devices  10.6 us (2%)
    all_gather x4, waiting for transfers between devices, on_device(): values = all_gather(local_vals, ('gx', 'gy')).sum(axis=0)  384 us
    gather x4, local copies, waits for them, and re-layouts, on_device(): picked = jnp.take(flat_first, obs_cell[batch], axis=1)  65.2 us
    reduce_sum x4, other arithmetic, observation_terms(): ybar = jnp.mean(values, axis=0)  22.1 us
    dot_general x4, matrix products, apply_mixing(): jnp.dot(mixing.T, prime, precision=lax.Precision.HIGHEST)  21.6 us
    reduce_sum x4, other arithmetic, on_device(): values = all_gather(local_vals, ('gx', 'gy')).sum(axis=0)  20.8 us
    unnamed x74, local copies, waits for them, and re-layouts  20.1 us
    select_n x4, other arithmetic, on_device(): local_vals = jnp.where(owned, picked, 0.0)  15.5 us
  transfers between devices with their start and end apart: 8, of which 6 were waited for; matrix products, arithmetic and copies ran while one was open for 2% of the time, Pallas kernels for 0%

profile of v1, /device:TPU:0, one launch (start us, length us, event | category | flops | bytes accessed | tf_op | source)
XLA Modules:
  0.0 653.5 jit_solution(10514645233891234021)
XLA Ops:
  7.2 4.6 copy.121
  28.5 4.9 collective-permute-start.3
  33.6 6.3 collective-permute-done.2
  41.7 9.1 %select_maximum_fusion = f32[24,4,10,10,130]{4,1,3,2,0:T(4,128)S(1)} fusion(f32[24,4,10,1,128]{4,1,3,2,0:T(4,128)S(1)} %collective-permute-done.2, f32[24,4,10,8,128]{4,1,3,2,0:T(4,128)} %copy-done.6, f32[24,4,10,1,128]{4,1,3,2,0:T(4,128)S(1)} %collective-permute-done.3), kind=kLoop, calls=%fused_computation.10 | loop fusion | flops 9984000 | bytes 9907200 | tf_op jit(solution)/shard_map/concatenate | solution.py:20
  50.9 13.2 %fusion.70 = (f32[4,8,8,128]{3,0,2,1:T(4,128)S(1)}, f32[24,4,8,8,128]{4,1,3,2,0:T(4,128)S(1)}) fusion(f32[24,4,8,8,128]{4,1,3,2,0:T(4,128)S(1)} %copy-done.9, f32[128]{0:T(128)S(1)} %compare_convert_fusion, f32[24,8,8]{2,1,0:T(8,128)S(1)} %copy.119, f32[4,4]{1,0:T(4,128)S(1)} %copy-done, f32[24,4,10,10,130]{4,1,3,2,0:T(4,128)S(1)} %select_maximum_fusion, ...), kind=kOutput, calls=%fused_computation.151 | convolution fusion | flops 55017472 | bytes 21662208 | tf_op jit(solution)/shard_map/fg,mgxyz->mfxyz/dot_general | solution.py:32
  66.5 3.1 copy.135
  69.6 16.3 %gather_fusion = f32[4096,24]{1,0:T(8,128)} fusion(f32[24,8192]{0,1:T(8,128)} %bitcast.99, s32[4096]{0:T(1024)S(1)} %fusion.55), kind=kCustom, calls=%fused_computation.clone | custom fusion | bytes 802816 | tf_op jit(solution)/shard_map/jit(_take)/gather | solution.py:83
  85.9 3.2 bitcast_select_fusion.3
  96.0 106.6 %all-gather.9.cloned.1.call-done = f32[768,4096]{1,0:T(8,128)} async-done(((f32[24,4096]{1,0:T(8,128)}), f32[768,4096]{1,0:T(8,128)}) %all-gather.9.cloned.1.call-update) | async-done | bytes 12582928 | tf_op jit(solution)/shard_map/all_gather | solution.py:87
  202.6 5.2 reduce_sum.181
  208.4 5.2 reduce_sum.180
  216.8 7.3 %fusion.71 = (f32[32768]{0:T(1024)S(1)}, f32[24,32768]{1,0:T(8,128)S(1)}) fusion(f32[24,24]{1,0:T(8,128)S(1)} %convolution_multiply_fusion.3, f32[3,8,256,128]{3,2,1,0:T(8,128)S(1)} %bitcast.103, f32[32768]{0:T(1024)} %bitcast.108), kind=kOutput, calls=%fused_computation.152 | convolution fusion | flops 228818944 | bytes 6555904 | tf_op jit(solution)/shard_map/dot_general | solution.py:56
  228.5 16.3 %gather_fusion.1 = f32[4096,24]{1,0:T(8,128)} fusion(f32[24,8192]{0,1:T(8,128)} %bitcast.100, s32[4096]{0:T(1024)S(1)} %copy-done.19), kind=kCustom, calls=%fused_computation.1.clone | custom fusion | bytes 802816 | tf_op jit(solution)/shard_map/jit(_take)/gather | solution.py:83
  244.7 3.2 bitcast_select_fusion.2
  249.7 93.9 %all-gather.11.cloned.1.call-done = f32[768,4096]{1,0:T(8,128)} async-done(((f32[24,4096]{1,0:T(8,128)}), f32[768,4096]{1,0:T(8,128)}) %all-gather.11.cloned.1.call-update) | async-done | bytes 12582928 | tf_op jit(solution)/shard_map/all_gather | solution.py:87
  343.7 5.2 reduce_sum.184
  348.9 5.2 reduce_sum.185
  355.7 6.0 fusion.72
  363.2 3.5 copy.128
  366.7 16.4 %gather_fusion.2 = f32[4096,24]{1,0:T(8,128)} fusion(f32[24,8192]{0,1:T(8,128)} %bitcast.101, s32[4096]{0:T(1024)S(1)} %fusion.57), kind=kCustom, calls=%fused_computation.2.clone | custom fusion | bytes 802816 | tf_op jit(solution)/shard_map/jit(_take)/gather | solution.py:83
  383.1 6.0 bitcast_select_fusion.1
  389.1 2.9 copy.129
  394.7 91.7 %all-gather.13.cloned.1.call-done = f32[768,4096]{1,0:T(8,128)} async-done(((f32[24,4096]{1,0:T(8,128)}), f32[768,4096]{1,0:T(8,128)}) %all-gather.13.cloned.1.call-update) | async-done | bytes 12582928 | tf_op jit(solution)/shard_map/all_gather | solution.py:87
  486.5 5.2 reduce_sum.188
  491.7 5.8 reduce_sum.189
  500.5 4.3 fusion.73
  509.4 16.3 %gather_fusion.3 = f32[4096,24]{1,0:T(8,128)} fusion(f32[24,8192]{0,1:T(8,128)} %bitcast.102, s32[4096]{0:T(1024)S(1)} %copy-done.20), kind=kCustom, calls=%fused_computation.3.clone | custom fusion | bytes 802816 | tf_op jit(solution)/shard_map/jit(_take)/gather | solution.py:83
  525.8 3.2 bitcast_select_fusion
  532.8 91.9 %all-gather.15.cloned.1.call-done = f32[768,4096]{1,0:T(8,128)} async-done(((f32[24,4096]{1,0:T(8,128)}), f32[768,4096]{1,0:T(8,128)}) %all-gather.15.cloned.1.call-update) | async-done | bytes 12582928 | tf_op jit(solution)/shard_map/all_gather | solution.py:87
  624.7 5.2 reduce_sum.192
  629.9 5.9 reduce_sum.193
  640.4 4.1 fusion.14
  (156 shorter events, 61.6 us)
Async XLA Ops:
  7.2 43.7 %copy-start = (f32[4,4]{1,0:T(4,128)S(1)}, f32[4,4]{1,0:T(4,128)}, u32[]{:S(2)}) copy-start(f32[4,4]{1,0:T(4,128)} %param.12) | copy-start | bytes 196
  7.2 14.2 %copy-start.5 = (f32[24,4,8,8,128]{4,3,2,1,0:T(8,128)S(1)}, f32[24,4,8,8,128]{4,3,2,1,0:T(8,128)}, u32[]{:S(2)}) copy-start(f32[24,4,8,8,128]{4,3,2,1,0:T(8,128)} %param.10) | copy-start | bytes 9437188
  7.2 195.4 %all-gather.9.cloned.1.call-start = ((), (), s32[]{:S(2)}) async-start(), calls=%async_computation | async-start | bytes 12976128 | tf_op jit(solution)/shard_map/all_gather | solution.py:87
  7.2 10.9 %copy-start.21 = (s32[4,4096]{1,0:T(4,128)S(1)}, s32[4,4096]{1,0:T(4,128)}, u32[]{:S(2)}) copy-start(s32[4,4096]{1,0:T(4,128)} %param.14) | copy-start | bytes 196612
  14.4 6.1 collective-permute-start.1
  16.8 7.3 %collective-permute-start = (f32[24,4,1,8,128]{4,1,3,2,0:T(4,128)}, f32[24,4,1,8,128]{4,1,3,2,0:T(4,128)}, u32[]{:S(2)}, u32[]{:S(2)}) collective-permute-start(f32[24,4,1,8,128]{4,1,3,2,0:T(4,128)} %get-tuple-element.11), channel_id=1, source_target_pairs={{4,0},{8,4},{12,8},{16,12},{20,16},{24,20},{28,24},{5,1},{9,5},{13... | collective-permute-start | bytes 1179656 | tf_op jit(solution)/shard_map/ppermute | solution.py:19
  21.3 12.1 %copy-start.11 = (f32[24,8,8]{0,2,1:T(8,128)S(1)}, f32[24,8,8]{0,2,1:T(8,128)}, u32[]{:S(2)}) copy-start(f32[24,8,8]{0,2,1:T(8,128)} %param.11) | copy-start | bytes 18436
  21.4 12.2 %copy-start.18 = (s32[1,4096]{1,0:T(1,128)S(1)}, s32[1,4096]{1,0:T(1,128)}, u32[]{:S(2)}) copy-start(s32[1,4096]{1,0:T(1,128)} %get-tuple-element.23) | copy-start | bytes 49156
  27.2 12.7 %collective-permute-start.2 = (f32[24,4,10,1,128]{4,1,3,2,0:T(4,128)S(1)}, f32[24,4,10,1,128]{4,1,3,2,0:T(4,128)S(1)}, u32[]{:S(2)}, u32[]{:S(2)}) collective-permute-start(f32[24,4,10,1,128]{4,1,3,2,0:T(4,128)S(1)} %get-tuple-element.10), channel_id=1, source_target_pairs={{1,0},{2,1},{3,2},{5,4},{6,5},{7,6},{9,8},{10,9},{11,10},{13,12},{... | collective-permute-start | bytes 1474568 | tf_op jit(solution)/shard_map/ppermute | solution.py:19
  28.5 13.2 %collective-permute-start.3 = (f32[24,4,10,1,128]{4,1,3,2,0:T(4,128)S(1)}, f32[24,4,10,1,128]{4,1,3,2,0:T(4,128)S(1)}, u32[]{:S(2)}, u32[]{:S(2)}) collective-permute-start(f32[24,4,10,1,128]{4,1,3,2,0:T(4,128)S(1)} %get-tuple-element.9), channel_id=1, source_target_pairs={{0,1},{1,2},{2,3},{4,5},{5,6},{6,7},{8,9},{9,10},{10,11},{12,13},{... | collective-permute-start | bytes 1474568 | tf_op jit(solution)/shard_map/ppermute | solution.py:16
  33.6 17.3 %copy-start.7 = (f32[24,4,10,8,128]{4,1,3,2,0:T(4,128)S(1)}, f32[24,4,10,8,128]{4,1,3,2,0:T(4,128)}, u32[]{:S(2)}) copy-start(f32[24,4,10,8,128]{4,1,3,2,0:T(4,128)} %copy-done.6) | copy-start | bytes 11796484
  33.6 17.3 %copy-start.9 = (f32[24,4,8,8,128]{4,1,3,2,0:T(4,128)S(1)}, f32[24,4,8,8,128]{4,1,3,2,0:T(4,128)}, u32[]{:S(2)}) copy-start(f32[24,4,8,8,128]{4,1,3,2,0:T(4,128)} %copy-done.8) | copy-start | bytes 9437188
  33.6 17.3 %copy-start.14 = (f32[24,4,1,8,128]{4,1,3,2,0:T(4,128)S(1)}, f32[24,4,1,8,128]{4,1,3,2,0:T(4,128)}, u32[]{:S(2)}) copy-start(f32[24,4,1,8,128]{4,1,3,2,0:T(4,128)} %copy-done.13) | copy-start | bytes 1179652
  85.9 5.1 copy-start.32
  85.9 6.4 copy-start.17
  90.5 253.2 %all-gather.11.cloned.1.call-start = ((), (), s32[]{:S(2)}) async-start(), calls=%async_computation.1 | async-start | bytes 12976128 | tf_op jit(solution)/shard_map/all_gather | solution.py:87
  216.8 7.3 %copy-start.25 = (f32[24,24]{1,0:T(8,128)}, f32[24,24]{1,0:T(8,128)S(1)}, u32[]{:S(2)}) copy-start(f32[24,24]{1,0:T(8,128)S(1)} %convolution_multiply_fusion.3) | copy-start | bytes 6916
  244.7 4.9 copy-start.16
  249.3 237.1 %all-gather.13.cloned.1.call-start = ((), (), s32[]{:S(2)}) async-start(), calls=%async_computation.2 | async-start | bytes 12976128 | tf_op jit(solution)/shard_map/all_gather | solution.py:87
  363.2 19.9 %copy-start.28 = (pred[4096]{0:T(1024)(128)(4,1)S(1)}, pred[4096]{0:T(1024)(128)(4,1)}, u32[]{:S(2)}) copy-start(pred[4096]{0:T(1024)(128)(4,1)} %get-tuple-element.8) | copy-start | bytes 12292
  383.1 9.0 %copy-start.31 = (f32[64]{0:T(128)S(1)}, f32[64]{0:T(128)}, u32[]{:S(2)}) copy-start(f32[64]{0:T(128)} %get-tuple-element.28) | copy-start | bytes 772
  383.1 9.8 %copy-start.15 = (s32[1,4096]{1,0:T(1,128)S(1)}, s32[1,4096]{1,0:T(1,128)}, u32[]{:S(2)}) copy-start(s32[1,4096]{1,0:T(1,128)} %get-tuple-element.21) | copy-start | bytes 49156
  392.0 232.6 %all-gather.15.cloned.1.call-start = ((), (), s32[]{:S(2)}) async-start(), calls=%async_computation.3 | async-start | bytes 12976128 | tf_op jit(solution)/shard_map/all_gather | solution.py:87
  500.5 4.3 copy-start.22
  506.6 19.1 %copy-start.27 = (pred[4096]{0:T(1024)(128)(4,1)S(1)}, pred[4096]{0:T(1024)(128)(4,1)}, u32[]{:S(2)}) copy-start(pred[4096]{0:T(1024)(128)(4,1)} %get-tuple-element.5) | copy-start | bytes 12292
  506.6 19.1 %copy-start.29 = (pred[4096]{0:T(1024)(128)(4,1)S(1)}, pred[4096]{0:T(1024)(128)(4,1)}, u32[]{:S(2)}) copy-start(pred[4096]{0:T(1024)(128)(4,1)} %compare_and_fusion) | copy-start | bytes 12292
  525.7 4.6 copy-start.12
  525.7 4.9 copy-start.30
  525.7 5.6 copy-start.26
  525.7 6.1 copy-start.23
  629.9 10.5 %copy-start.4 = (f32[24,32768]{1,0:T(8,128)S(1)}, f32[24,32768]{1,0:T(8,128)}, u32[]{:S(2)}) copy-start(f32[24,32768]{1,0:T(8,128)} %copy-done.3) | copy-start | bytes 9437188
  640.4 6.3 copy-start.1
  (9 other events, 15.5 us)
Sparse Core Ops, SparseCore 0:
  90.6 111.9 all-gather.8
  249.4 94.1 all-gather.10
  392.2 94.2 all-gather.12
  530.4 94.1 all-gather.14
